TPU v7x, 256 devices: a whole 4x4x8 slice. The times are simulated.
256 devices in a mesh: seq: 32 (over y, x, core), head: 8 (over z).
Axes of the slice: x: 4, y: 4, z: 8, core: 2. Of those that a mesh axis runs over, the one named last changes fastest.
Arguments:
- query_in: bfloat16 [16384, 2048], P(('seq', 'head')), may hold values from -6 to 6
- key_in: bfloat16 [16384, 2048], P(('seq', 'head')), may hold values from -6 to 6
- value_in: bfloat16 [16384, 4096], P(('seq', 'head')), may hold values from -6 to 6
- gate_in: bfloat16 [16384, 4096], P(('seq', 'head')), may hold values from -6 to 6
- write_strength: bfloat16 [16384, 32], P(('seq', 'head')), may hold values from 0.0003 to 0.9
- log_decay: bfloat16 [16384, 32], P(('seq', 'head')), may hold values from -0.9 to 0
- conv_weight: bfloat16 [4, 8192], replicated, may hold values from -3 to 3
- norm_gain: float32 [128], replicated, may hold values from 0.1 to 1.9
Outputs:
- mixed: bfloat16 [16384, 4096], P(('seq', 'head'))
All inputs are finite; a program needn't handle non-finite values.
Results may differ from a plain program's by a relative error of at most 0.0057.
Values may be sent and summed in bfloat16 or wider, within the bound.
A program may use at most 128 MiB of HBM per device.

v0:
```python
import functools

import jax
import jax.numpy as jnp
from jax import lax
from jax.experimental import pallas as pl
from jax.experimental.pallas import tpu as pltpu
from jax.sharding import PartitionSpec as P

MESH = pl.DeviceIdType.MESH
F32 = jnp.float32
BF16 = jnp.bfloat16
EPSILON = 1e-06

GROUPS = 8
TOK = 64
LINE = 8
LINES = 4
SEQ = LINE * LINES
HEADS = 4
D = 128
C = 128
ROWS = TOK * GROUPS
CHUNKS = ROWS // C
RIM = 16

NN = (((1,), (0,)), ((), ()))
NT = (((1,), (1,)), ((), ()))
TN = (((0,), (0,)), ((), ()))


def dot(a, b, dims=NN):
    return lax.dot_general(a, b, dims, preferred_element_type=F32)


def split(x):
    high = x.astype(BF16)
    return high, (x - high.astype(F32)).astype(BF16)


def mm3(a, b, dims=NN):
    a1, a2 = split(a)
    b1, b2 = split(b)
    return dot(a1, b1, dims) + (dot(a1, b2, dims) + dot(a2, b1, dims))


def mm2l(a, b, dims=NN):
    a1, a2 = split(a)
    return dot(a1, b, dims) + dot(a2, b, dims)


def mm2r(a, b, dims=NN):
    b1, b2 = split(b)
    return dot(a, b1, dims) + dot(a, b2, dims)


def mm1(a, b, dims=NN):
    return dot(a.astype(BF16), b.astype(BF16), dims)


def silu(x):
    return x / (1.0 + jnp.exp(-x))


def conv(buf, start, taps):
    x = buf[pl.ds(start, C + RIM), :].astype(F32)
    total = x[RIM - 3 : RIM - 3 + C] * taps[0:1]
    for j in range(1, 4):
        total = total + x[RIM - 3 + j : RIM - 3 + j + C] * taps[j : j + 1]
    return silu(total).astype(BF16)


def unit_inverse(lower, rows, cols):
    t = jnp.where(rows == cols, 1.0, 0.0).reshape(C // 8, 8, C)
    base = (rows // 8) * 8
    for j in range(7):
        factor = jnp.sum(jnp.where(cols == base + j, lower, 0.0), axis=1, keepdims=True)
        t = t - factor.reshape(C // 8, 8, 1) * t[:, j : j + 1, :]
    t = t.reshape(C, C)
    size = 8
    while size < C:
        below = (rows // size == cols // size + 1) & (rows // size % 2 == 1)
        part = jnp.where(below, lower, 0.0)
        t = t - mm3(t, mm3(part, t))
        size *= 2
    return t


def kernel(
    q_in, k_in, v_in, gate_in, ws_in, ld_in, w_in, gain_ref, out_ref,
    qbuf, kbuf, vbuf, gate, ws, ld, wbuf, gb_send, gb_recv,
    kc, fs, tinv, ew, mc, ac, pre, m_send, a_send, m_recv, a_recv,
    mpre, msuf, apre, ym_send, ya_send, ym_recv, ya_recv, h_send, h_recv, pb, o_send, o_recv,
    local_sem, send_sem, recv_sem,
):
    s = lax.axis_index("seq")
    z = lax.axis_index("head")
    y = s // LINE
    l = lax.rem(s, LINE)

    def at_head(d):
        return lax.rem(z + d, GROUPS)

    def at_line(d):
        return lax.rem(l + d, LINE)

    barrier = pltpu.get_barrier_semaphore()
    for d in range(1, GROUPS):
        pl.semaphore_signal(barrier, inc=1, device_id=(s, at_head(d)), device_id_type=MESH)
    for d in range(1, LINE):
        pl.semaphore_signal(barrier, inc=1, device_id=(y * LINE + at_line(d), z), device_id_type=MESH)
    for d in range(1, LINES):
        pl.semaphore_signal(
            barrier, inc=1, device_id=(lax.rem(y + d, LINES) * LINE + l, z), device_id_type=MESH
        )
    pl.semaphore_signal(barrier, inc=1, device_id=(lax.rem(s + SEQ - 1, SEQ), z), device_id_type=MESH)

    mine = pl.ds(pl.multiple_of(RIM + z * TOK, RIM), TOK)

    def own_columns(width):
        return pl.ds(pl.multiple_of(z * width, width), width)

    copies = [
        pltpu.make_async_copy(ws_in, ws, local_sem.at[0]),
        pltpu.make_async_copy(ld_in, ld, local_sem.at[1]),
        pltpu.make_async_copy(w_in, wbuf, local_sem.at[2]),
        pltpu.make_async_copy(k_in.at[:, own_columns(256)], kbuf.at[mine, :], local_sem.at[3]),
        pltpu.make_async_copy(v_in.at[:, own_columns(512)], vbuf.at[mine, :], local_sem.at[4]),
        pltpu.make_async_copy(q_in.at[:, own_columns(256)], qbuf.at[mine, :], local_sem.at[5]),
        pltpu.make_async_copy(gate_in, gate, local_sem.at[6]),
    ]
    for copy in copies:
        copy.start()

    rows = lax.broadcasted_iota(jnp.int32, (C, C), 0)
    cols = lax.broadcasted_iota(jnp.int32, (C, C), 1)
    eye = rows == cols
    tril = rows >= cols
    strict = rows > cols

    copies[0].wait()
    copies[1].wait()
    upto = jnp.where(tril[:TOK, :TOK], 1.0, 0.0).astype(BF16)
    running = dot(upto, ld[...])
    both = jnp.concatenate([ws[...].astype(F32), running], axis=1)
    both = jnp.concatenate([both, both], axis=0).T
    for g in range(GROUPS):
        gb_send[g] = jnp.concatenate(
            [both[HEADS * g : HEADS * g + HEADS], both[32 + HEADS * g : 32 + HEADS * g + HEADS]], axis=0
        )
    pl.semaphore_wait(barrier, GROUPS - 1 + LINE - 1 + LINES - 1 + 1)

    def to_head(kind, d, src, dst):
        return pltpu.make_async_remote_copy(
            src_ref=src,
            dst_ref=dst,
            send_sem=send_sem.at[kind, d],
            recv_sem=recv_sem.at[kind, d],
            device_id=(s, at_head(d)),
            device_id_type=MESH,
        )

    def to_seq(kind, d, target, src, dst):
        return pltpu.make_async_remote_copy(
            src_ref=src,
            dst_ref=dst,
            send_sem=send_sem.at[kind, d],
            recv_sem=recv_sem.at[kind, d],
            device_id=(target, z),
            device_id_type=MESH,
        )

    def columns_to(d, width):
        return pl.ds(pl.multiple_of(at_head(d) * width, width), width)

    order = [4, 3, 5, 2, 6, 1, 7]
    k_copies, v_copies, q_copies, g_copies = [], [], [], []
    for d in order:
        g_copies.append(to_head(0, d, gb_send.at[at_head(d)], gb_recv.at[z]))
        k_copies.append(to_head(1, d, k_in.at[:, columns_to(d, 256)], kbuf.at[mine, :]))
    for d in order:
        v_copies.append(to_head(2, d, v_in.at[:, columns_to(d, 512)], vbuf.at[mine, :]))
    for d in order:
        q_copies.append(to_head(3, d, q_in.at[:, columns_to(d, 256)], qbuf.at[mine, :]))
    for copy in g_copies + k_copies + v_copies + q_copies:
        copy.start()
    gb_recv[z] = gb_send[z]

    following = lax.rem(s + 1, SEQ)

    def rim_copy(index, buf):
        return to_seq(4, index, following, buf.at[pl.ds(ROWS, RIM), :], buf.at[pl.ds(0, RIM), :])

    def arrived(own, others, index, buf):
        own.wait()
        for copy in others:
            copy.wait_recv()
        rim = rim_copy(index, buf)
        rim.start()
        return rim

    def rim_arrived(rim, buf):
        rim.wait_recv()

        @pl.when(s == 0)
        def _():
            buf[pl.ds(0, RIM), :] = jnp.zeros((RIM, buf.shape[1]), BF16)

    def chunk_scales(c):
        first, second = gb_recv[2 * c], gb_recv[2 * c + 1]
        lane = lax.broadcasted_iota(jnp.int32, (8, C), 1)
        sub = lax.broadcasted_iota(jnp.int32, (8, C), 0)
        carry = jnp.where(sub >= HEADS, first[:, TOK - 1 : TOK], 0.0)
        across = jnp.where(lane < TOK, first, second + carry)
        return across, across.T

    copies[2].wait()
    for copy in g_copies:
        copy.wait_recv()
    k_rim = arrived(copies[3], k_copies, 0, kbuf)
    rim_arrived(k_rim, kbuf)
    taps_k = wbuf[:, pl.ds(pl.multiple_of(2048 + z * 256, 256), 256)].astype(F32)

    def key_body(i, carry):
        c = lax.rem(i + 1, CHUNKS)
        start = pl.multiple_of(c * C, C)
        block = pl.ds(start, C)
        keys = conv(kbuf, start, taps_k)
        kc[block, :] = keys
        across, down = chunk_scales(c)
        for kh in range(2):
            key = keys[:, kh * D : (kh + 1) * D]
            kk = dot(key, key, NT)
            diagonal = jnp.where(eye, kk, 0.0)
            s_col = lax.rsqrt(jnp.sum(diagonal, axis=1, keepdims=True) + EPSILON)
            s_row = lax.rsqrt(jnp.sum(diagonal, axis=0, keepdims=True) + EPSILON)
            for j in range(2):
                h = kh * 2 + j
                b_col, c_col = down[:, h : h + 1], down[:, HEADS + h : HEADS + h + 1]
                b_row, c_row = across[h : h + 1], across[HEADS + h : HEADS + h + 1]
                fade = jnp.where(tril, jnp.exp(jnp.where(tril, c_col - c_row, 0.0)), 0.0) * s_row
                fs[h, block, :] = fade
                lower = jnp.where(strict, kk * fade * (s_col * b_col), 0.0)
                t = unit_inverse(lower, rows, cols) * b_row
                tinv[h, block, :] = t
                erase = mm2l(t * (s_row * jnp.exp(c_row)), key)
                ew[h, block, pl.ds(0, D)] = erase
                end = c_row[:, C - 1 : C]
                taken = mm2r(key, erase * (s_col * jnp.exp(end - c_col)), TN)
                mc[h, c] = jnp.where(eye, jnp.exp(end), 0.0) - taken
        return carry

    lax.fori_loop(0, CHUNKS, key_body, 0)

    identity = jnp.where(eye, 1.0, 0.0)
    left, right = pl.ds(0, D), pl.ds(D, D)
    for h in range(HEADS):
        pre[h, 0, :, left] = identity
        pre[h, 0, :, right] = jnp.zeros((D, D), F32)
        running = mc[h, 0]
        for c in range(1, CHUNKS):
            pre[h, c, :, left] = running
            running = mm3(mc[h, c], running)
        m_send[h] = running

    def unit_head(u):
        return u // 2

    def unit_half(u):
        return pl.ds(pl.multiple_of(lax.rem(u, 2) * 64, 64), 64)

    m_copies, a_copies, h_copies = [], [], []
    for d in range(1, LINE):
        u = at_line(d)
        target = y * LINE + u
        m_copies.append(to_seq(5, d, target, m_send.at[unit_head(u)], m_recv.at[l]))
        a_copies.append(to_seq(6, d, target, a_send.at[unit_head(u), unit_half(u), :], a_recv.at[l]))
        h_copies.append(to_seq(7, d, target, h_send.at[u], h_recv.at[l]))
    for copy in m_copies:
        copy.start()
    m_recv[l] = m_send[unit_head(l)]

    v_rim = arrived(copies[4], v_copies, 1, vbuf)
    rim_arrived(v_rim, vbuf)
    taps_v = wbuf[:, pl.ds(pl.multiple_of(4096 + z * 512, 512), 512)].astype(F32)

    def value_body(c, carry):
        start = pl.multiple_of(c * C, C)
        block = pl.ds(start, C)
        values = conv(vbuf, start, taps_v)
        across, down = chunk_scales(c)
        for kh in range(2):
            key = kc[block, pl.ds(kh * D, D)]
            key32 = key.astype(F32)
            s_col = lax.rsqrt(jnp.sum(key32 * key32, axis=1, keepdims=True) + EPSILON)
            for j in range(2):
                h = kh * 2 + j
                c_col = down[:, HEADS + h : HEADS + h + 1]
                end = across[HEADS + h : HEADS + h + 1, C - 1 : C]
                write = mm2l(tinv[h, block, :], values[:, h * D : (h + 1) * D])
                ew[h, block, pl.ds(D, D)] = write
                ac[h, c] = mm2r(key, write * (s_col * jnp.exp(end - c_col)), TN)
        return carry

    lax.fori_loop(0, CHUNKS, value_body, 0)
    for h in range(HEADS):
        running = ac[h, 0]
        for c in range(1, CHUNKS):
            pre[h, c, :, right] = running
            running = mm3(mc[h, c], running) + ac[h, c]
        a_send[h] = running.T
    for copy in a_copies:
        copy.start()
    a_recv[l] = a_send[unit_head(l), unit_half(l), :]

    for copy in m_copies:
        copy.wait_recv()
    running = m_recv[0]
    for i in range(1, LINE):
        mpre[i] = running
        running = mm3(m_recv[i], running)
    ym_send[...] = running
    ym_copies, ya_copies = [], []
    for d in range(1, LINES):
        target = lax.rem(y + d, LINES) * LINE + l
        ym_copies.append(to_seq(8, d, target, ym_send, ym_recv.at[d - 1]))
        ya_copies.append(to_seq(9, d, target, ya_send, ya_recv.at[d - 1]))
    for copy in ym_copies:
        copy.start()
    running = m_recv[LINE - 1]
    for i in range(LINE - 2, -1, -1):
        msuf[i] = running
        if i:
            running = mm3(running, m_recv[i])

    for copy in a_copies:
        copy.wait_recv()
    total = a_recv[LINE - 1]
    for i in range(LINE - 1):
        total = total + mm3(a_recv[i], msuf[i], NT)
    ya_send[...] = total
    for copy in ya_copies:
        copy.start()

    running = a_recv[0]
    for i in range(1, LINE):
        apre[i] = running
        if i < LINE - 1:
            running = mm3(running, m_recv[i], NT) + a_recv[i]

    for copy in ym_copies:
        copy.wait_recv()
    across_two = mm3(ym_recv[0], ym_recv[1])
    for copy in ya_copies:
        copy.wait_recv()
    entering = jnp.where(y >= 1, ya_recv[0], 0.0)
    entering = entering + jnp.where(y >= 2, mm3(ya_recv[1], ym_recv[0], NT), 0.0)
    entering = entering + jnp.where(y >= 3, mm3(ya_recv[2], across_two, NT), 0.0)
    h_send[0] = entering
    for i in range(1, LINE):
        h_send[i] = mm3(entering, mpre[i], NT) + apre[i]
    for copy in h_copies:
        copy.start()
    h_recv[l] = h_send[l]

    q_rim = arrived(copies[5], q_copies, 2, qbuf)
    rim_arrived(q_rim, qbuf)
    taps_q = wbuf[:, pl.ds(pl.multiple_of(z * 256, 256), 256)].astype(F32)

    def query_body(c, carry):
        start = pl.multiple_of(c * C, C)
        block = pl.ds(start, C)
        queries = conv(qbuf, start, taps_q)
        across, down = chunk_scales(c)
        for kh in range(2):
            key = kc[block, pl.ds(kh * D, D)]
            query = queries[:, kh * D : (kh + 1) * D]
            query32 = query.astype(F32)
            s_col = lax.rsqrt(jnp.sum(query32 * query32, axis=1, keepdims=True) + EPSILON) * (D**-0.5)
            qk = dot(query, key, NT) * s_col
            for j in range(2):
                h = kh * 2 + j
                c_col = down[:, HEADS + h : HEADS + h + 1]
                inner = mm3(qk * fs[h, block, :], ew[h, block, :])
                reads = query32 * (s_col * jnp.exp(c_col)) - inner[:, :D]
                outer = mm3(reads, pre[h, c])
                pb[h, block, left] = outer[:, :D]
                pb[h, block, right] = outer[:, D:] + inner[:, D:]
        return carry

    lax.fori_loop(0, CHUNKS, query_body, 0)

    for copy in h_copies:
        copy.wait_recv()
    o_copies = []
    for d in range(1, GROUPS):
        o_copies.append(to_head(10, d, o_send.at[at_head(d)], o_recv.at[z]))

    def out_rows(t):
        block = pl.ds(pl.multiple_of(t * TOK, TOK), TOK)
        for h in range(HEADS):
            state = jnp.concatenate([h_recv[2 * h], h_recv[2 * h + 1]], axis=0)
            o = mm3(pb[h, block, left], state, NT) + pb[h, block, right]
            o_send[t, :, pl.ds(h * D, D)] = o.astype(BF16)

    for copy, d in zip(o_copies, range(1, GROUPS)):
        out_rows(at_head(d))
        copy.start()
    out_rows(z)
    o_recv[z] = o_send[z]

    copies[6].wait()
    for copy in o_copies:
        copy.wait_recv()
    gain = gain_ref[...]

    def norm_body(g, carry):
        for h in range(HEADS):
            a = o_recv[g, :, pl.ds(h * D, D)].astype(F32)
            a = a * lax.rsqrt(jnp.mean(a * a, axis=1, keepdims=True) + EPSILON)
            here = pl.ds(pl.multiple_of(g * 512 + h * D, D), D)
            out_ref[:, here] = (a * gain * silu(gate[:, here].astype(F32))).astype(BF16)
        return carry

    lax.fori_loop(0, GROUPS, norm_body, 0)

    for copy in g_copies + k_copies + v_copies + q_copies + [k_rim, v_rim, q_rim]:
        copy.wait_send()
    for copy in m_copies + a_copies + h_copies + ym_copies + ya_copies + o_copies:
        copy.wait_send()


def local(query_in, key_in, value_in, gate_in, write_strength, log_decay, conv_weight, norm_gain):
    anywhere = pl.BlockSpec(memory_space=pl.ANY)
    vmem = pl.BlockSpec(memory_space=pltpu.VMEM)
    return pl.pallas_call(
        kernel,
        out_shape=jax.ShapeDtypeStruct((TOK, 4096), BF16),
        in_specs=[anywhere] * 7 + [vmem],
        out_specs=vmem,
        scratch_shapes=[
            pltpu.VMEM((RIM + ROWS, 256), BF16),
            pltpu.VMEM((RIM + ROWS, 256), BF16),
            pltpu.VMEM((RIM + ROWS, 512), BF16),
            pltpu.VMEM((TOK, 4096), BF16),
            pltpu.VMEM((TOK, 32), BF16),
            pltpu.VMEM((TOK, 32), BF16),
            pltpu.VMEM((4, 8192), BF16),
            pltpu.VMEM((GROUPS, 8, C), F32),
            pltpu.VMEM((GROUPS, 8, C), F32),
            pltpu.VMEM((ROWS, 256), BF16),
            pltpu.VMEM((HEADS, ROWS, C), F32),
            pltpu.VMEM((HEADS, ROWS, C), F32),
            pltpu.VMEM((HEADS, ROWS, 2 * D), F32),
            pltpu.VMEM((HEADS, CHUNKS, D, D), F32),
            pltpu.VMEM((HEADS, CHUNKS, D, D), F32),
            pltpu.VMEM((HEADS, CHUNKS, D, 2 * D), F32),
            pltpu.VMEM((HEADS, D, D), F32),
            pltpu.VMEM((HEADS, D, D), F32),
            pltpu.VMEM((LINE, D, D), F32),
            pltpu.VMEM((LINE, 64, D), F32),
            pltpu.VMEM((LINE, D, D), F32),
            pltpu.VMEM((LINE, D, D), F32),
            pltpu.VMEM((LINE, 64, D), F32),
            pltpu.VMEM((D, D), F32),
            pltpu.VMEM((64, D), F32),
            pltpu.VMEM((LINES - 1, D, D), F32),
            pltpu.VMEM((LINES - 1, 64, D), F32),
            pltpu.VMEM((LINE, 64, D), F32),
            pltpu.VMEM((LINE, 64, D), F32),
            pltpu.VMEM((HEADS, ROWS, 2 * D), F32),
            pltpu.VMEM((GROUPS, TOK, 512), BF16),
            pltpu.VMEM((GROUPS, TOK, 512), BF16),
            pltpu.SemaphoreType.DMA((7,)),
            pltpu.SemaphoreType.DMA((11, 8)),
            pltpu.SemaphoreType.DMA((11, 8)),
        ],
        compiler_params=pltpu.CompilerParams(
            collective_id=0, has_side_effects=True, vmem_limit_bytes=48 * 1024 * 1024
        ),
    )(
        query_in, key_in, value_in, gate_in, write_strength, log_decay, conv_weight, norm_gain.reshape(1, D)
    )


def solution(mesh):
    rows = P(("seq", "head"), None)
    return jax.shard_map(
        local,
        mesh=mesh,
        in_specs=(rows, rows, rows, rows, rows, rows, P(), P()),
        out_specs=rows,
        check_vma=False,
    )
```

profile of v0, /device:TPU:1, one launch (start us, length us, event | category | flops | bytes accessed | tf_op | source)
XLA Modules:
  0.0 103.0 jit_solution(7680647759695950998)
XLA Ops:
  0.0 0.0 copy-start.6
  0.0 0.8 copy.9.ws_in
  0.8 0.0 copy-done.6
  0.8 0.0 copy-start.5
  0.8 0.1 copy.10.ld_in
  0.9 0.6 copy-done.5
  1.5 0.0 copy-start
  1.5 1.0 %copy-done = bf16[64,4096]{1,0:T(8,128)(2,1)S(1)} copy-done((bf16[64,4096]{1,0:T(8,128)(2,1)S(1)}, bf16[64,4096]{1,0:T(8,128)(2,1)}, u32[]{:S(2)}) %copy-start) | copy-done | bytes 524312
  2.5 0.0 copy-start.1
  2.5 1.0 %copy-done.1 = bf16[64,4096]{1,0:T(8,128)(2,1)S(1)} copy-done((bf16[64,4096]{1,0:T(8,128)(2,1)S(1)}, bf16[64,4096]{1,0:T(8,128)(2,1)}, u32[]{:S(2)}) %copy-start.1) | copy-done | bytes 524312
  3.6 0.0 copy-start.2
  3.6 0.9 copy-done.2
  4.5 0.0 copy-start.3
  4.5 0.9 copy-done.3
  5.5 0.0 copy-start.4
  5.5 0.8 copy-done.4
  6.3 95.9 %shard_map.82 = bf16[64,4096]{1,0:T(8,128)(2,1)S(1)} custom-call(bf16[64,2048]{1,0:T(8,128)(2,1)S(1)} %copy-done.2, bf16[64,2048]{1,0:T(8,128)(2,1)S(1)} %copy-done.3, bf16[64,4096]{1,0:T(8,128)(2,1)S(1)} %copy-done, bf16[64,4096]{1,0:T(8,128)(2,1)S(1)} %copy-done.1, bf16[64,32]{1,0:T(8,128)(2,1)S(1)} %copy.9.ws_in, bf16[64,32]{1,0:T(8,128)(2,1)S(1)} %copy.10.ld_in, ...), custom_call_target="tpu_custom_call" | custom-call | tf_op jit(solution)/shard_map/pallas_call | solution.py:436
  102.2 0.8 copy.12
Async XLA Ops:
  0.0 0.8 copy-start.6
  0.8 0.7 copy-start.5
  1.5 1.0 %copy-start = (bf16[64,4096]{1,0:T(8,128)(2,1)S(1)}, bf16[64,4096]{1,0:T(8,128)(2,1)}, u32[]{:S(2)}) copy-start(bf16[64,4096]{1,0:T(8,128)(2,1)} %v_in.1) | copy-start | bytes 1572868
  2.5 1.0 %copy-start.1 = (bf16[64,4096]{1,0:T(8,128)(2,1)S(1)}, bf16[64,4096]{1,0:T(8,128)(2,1)}, u32[]{:S(2)}) copy-start(bf16[64,4096]{1,0:T(8,128)(2,1)} %gate_in.1) | copy-start | bytes 1572868
  3.6 0.9 copy-start.2
  4.5 0.9 copy-start.3
  5.5 0.8 copy-start.4
where the time goes:
time: 103 us
  Pallas kernels  95.9 us (93%)
  local copies, waits for them, and re-layouts  7.07 us (7%)
    pallas_call x1, Pallas kernels, local(): pl.pallas_call(kernel, out_shape=jax.ShapeDtypeStruct((TOK, 4096), BF16),...  95.9 us
    unnamed x17, local copies, waits for them, and re-layouts  7.07 us

commit v1 on v0

--- a/solution.py
+++ b/solution.py
@@ -38,24 +38,33 @@
     return high, (x - high.astype(F32)).astype(BF16)
 
 
+def beside(b1, b2, dims):
+    return jnp.concatenate([b1, b2], axis=0 if dims == NT else 1)
+
+
+def mm2l(a, b, dims=NN):
+    a1, a2 = split(a)
+    axis = 1 if dims == NT else 0
+    return dot(jnp.concatenate([a1, a2], axis=1), jnp.concatenate([b, b], axis=axis), dims)
+
+
+def mm2r(a, b, dims=NN):
+    b1, b2 = split(b)
+    both = dot(a, beside(b1, b2, dims), dims)
+    half = both.shape[1] // 2
+    return both[:, :half] + both[:, half:]
+
+
 def mm3(a, b, dims=NN):
     a1, a2 = split(a)
     b1, b2 = split(b)
-    return dot(a1, b1, dims) + (dot(a1, b2, dims) + dot(a2, b1, dims))
-
-
-def mm2l(a, b, dims=NN):
-    a1, a2 = split(a)
-    return dot(a1, b, dims) + dot(a2, b, dims)
-
-
-def mm2r(a, b, dims=NN):
-    b1, b2 = split(b)
-    return dot(a, b1, dims) + dot(a, b2, dims)
-
-
-def mm1(a, b, dims=NN):
-    return dot(a.astype(BF16), b.astype(BF16), dims)
+    if b.shape[0 if dims == NT else 1] > D:
+        axis = 1 if dims == NT else 0
+        main = dot(jnp.concatenate([a1, a2], axis=1), jnp.concatenate([b1, b1], axis=axis), dims)
+        return main + dot(a1, b2, dims)
+    both = dot(a1, beside(b1, b2, dims), dims)
+    half = both.shape[1] // 2
+    return both[:, :half] + both[:, half:] + dot(a2, b1, dims)
 
 
 def silu(x):
@@ -70,25 +79,47 @@
     return silu(total).astype(BF16)
 
 
-def unit_inverse(lower, rows, cols):
-    t = jnp.where(rows == cols, 1.0, 0.0).reshape(C // 8, 8, C)
+def odd_blocks(x, size):
+    return jnp.concatenate([x[i : i + size] for i in range(size, C, 2 * size)], axis=0)
+
+
+def to_odd_blocks(x, size):
+    zero = jnp.zeros((size, x.shape[1]), x.dtype)
+    parts = []
+    for i in range(0, C // 2, size):
+        parts += [zero, x[i : i + size]]
+    return jnp.concatenate(parts, axis=0)
+
+
+def unit_inverses(lowers, rows, cols):
+    identity = jnp.where(rows == cols, 1.0, 0.0)
     base = (rows // 8) * 8
+    ts = [identity.reshape(C // 8, 8, C)] * len(lowers)
     for j in range(7):
-        factor = jnp.sum(jnp.where(cols == base + j, lower, 0.0), axis=1, keepdims=True)
-        t = t - factor.reshape(C // 8, 8, 1) * t[:, j : j + 1, :]
-    t = t.reshape(C, C)
+        picked = cols == base + j
+        for n, lower in enumerate(lowers):
+            factor = jnp.sum(jnp.where(picked, lower, 0.0), axis=1, keepdims=True).reshape(C // 8, 8, 1)
+            ts[n] = ts[n] - factor * ts[n][:, j : j + 1, :]
+    ts = [t.reshape(C, C) for t in ts]
     size = 8
     while size < C:
-        below = (rows // size == cols // size + 1) & (rows // size % 2 == 1)
-        part = jnp.where(below, lower, 0.0)
-        t = t - mm3(t, mm3(part, t))
+        below = odd_blocks(cols // size, size) == odd_blocks(rows // size, size) - 1
+        parts = [jnp.where(below, odd_blocks(lower, size), 0.0).astype(BF16) for lower in lowers]
+        firsts = [dot(part, t.astype(BF16)) for part, t in zip(parts, ts)]
+        seconds = [
+            dot(odd_blocks(t, size).astype(BF16), to_odd_blocks(first, size).astype(BF16))
+            for t, first in zip(ts, firsts)
+        ]
+        ts = [t - to_odd_blocks(second, size) for t, second in zip(ts, seconds)]
         size *= 2
-    return t
+    rounded = [t.astype(BF16) for t in ts]
+    misses = [identity - t.astype(F32) - mm2l(lower, t) for lower, t in zip(lowers, rounded)]
+    return [t.astype(F32) + dot(t, miss.astype(BF16)) for t, miss in zip(rounded, misses)]
 
 
 def kernel(
     q_in, k_in, v_in, gate_in, ws_in, ld_in, w_in, gain_ref, out_ref,
-    qbuf, kbuf, vbuf, gate, ws, ld, wbuf, gb_send, gb_recv,
+    qbuf, kbuf, vbuf, gate, gating, ws, ld, wbuf, gb_send, gb_recv,
     kc, fs, tinv, ew, mc, ac, pre, m_send, a_send, m_recv, a_recv,
     mpre, msuf, apre, ym_send, ya_send, ym_recv, ya_recv, h_send, h_recv, pb, o_send, o_recv,
     local_sem, send_sem, recv_sem,
@@ -140,10 +171,10 @@
 
     copies[0].wait()
     copies[1].wait()
-    upto = jnp.where(tril[:TOK, :TOK], 1.0, 0.0).astype(BF16)
-    running = dot(upto, ld[...])
-    both = jnp.concatenate([ws[...].astype(F32), running], axis=1)
-    both = jnp.concatenate([both, both], axis=0).T
+    upto = jnp.where(rows <= cols, 1.0, 0.0)[:TOK, :TOK].astype(BF16)
+    running = dot(ld[...], upto)
+    both = jnp.concatenate([ws[...].astype(F32), running], axis=0)
+    both = jnp.concatenate([both, both], axis=1)
     for g in range(GROUPS):
         gb_send[g] = jnp.concatenate(
             [both[HEADS * g : HEADS * g + HEADS], both[32 + HEADS * g : 32 + HEADS * g + HEADS]], axis=0
@@ -186,6 +217,16 @@
         copy.start()
     gb_recv[z] = gb_send[z]
 
+    copies[6].wait()
+    gain = jnp.concatenate([gain_ref[...]] * HEADS, axis=1)
+
+    def gate_body(g, carry):
+        here = pl.ds(pl.multiple_of(g * 512, 512), 512)
+        gating[:, here] = silu(gate[:, here].astype(F32)) * gain
+        return carry
+
+    lax.fori_loop(0, GROUPS, gate_body, 0)
+
     following = lax.rem(s + 1, SEQ)
 
     def rim_copy(index, buf):
@@ -218,36 +259,47 @@
     for copy in g_copies:
         copy.wait_recv()
     k_rim = arrived(copies[3], k_copies, 0, kbuf)
-    rim_arrived(k_rim, kbuf)
     taps_k = wbuf[:, pl.ds(pl.multiple_of(2048 + z * 256, 256), 256)].astype(F32)
 
     def key_body(i, carry):
         c = lax.rem(i + 1, CHUNKS)
+
+        @pl.when(i == CHUNKS - 1)
+        def _():
+            rim_arrived(k_rim, kbuf)
+
         start = pl.multiple_of(c * C, C)
         block = pl.ds(start, C)
         keys = conv(kbuf, start, taps_k)
         kc[block, :] = keys
         across, down = chunk_scales(c)
-        for kh in range(2):
-            key = keys[:, kh * D : (kh + 1) * D]
-            kk = dot(key, key, NT)
-            diagonal = jnp.where(eye, kk, 0.0)
-            s_col = lax.rsqrt(jnp.sum(diagonal, axis=1, keepdims=True) + EPSILON)
-            s_row = lax.rsqrt(jnp.sum(diagonal, axis=0, keepdims=True) + EPSILON)
-            for j in range(2):
-                h = kh * 2 + j
-                b_col, c_col = down[:, h : h + 1], down[:, HEADS + h : HEADS + h + 1]
-                b_row, c_row = across[h : h + 1], across[HEADS + h : HEADS + h + 1]
-                fade = jnp.where(tril, jnp.exp(jnp.where(tril, c_col - c_row, 0.0)), 0.0) * s_row
-                fs[h, block, :] = fade
-                lower = jnp.where(strict, kk * fade * (s_col * b_col), 0.0)
-                t = unit_inverse(lower, rows, cols) * b_row
-                tinv[h, block, :] = t
-                erase = mm2l(t * (s_row * jnp.exp(c_row)), key)
-                ew[h, block, pl.ds(0, D)] = erase
-                end = c_row[:, C - 1 : C]
-                taken = mm2r(key, erase * (s_col * jnp.exp(end - c_col)), TN)
-                mc[h, c] = jnp.where(eye, jnp.exp(end), 0.0) - taken
+        b_cols = [down[:, h : h + 1] for h in range(HEADS)]
+        c_cols = [down[:, HEADS + h : HEADS + h + 1] for h in range(HEADS)]
+        b_rows = [across[h : h + 1] for h in range(HEADS)]
+        c_rows = [across[HEADS + h : HEADS + h + 1] for h in range(HEADS)]
+        ends = [c_row[:, C - 1 : C] for c_row in c_rows]
+        key = [keys[:, kh * D : (kh + 1) * D] for kh in range(2)]
+        kk = [dot(part, part, NT) for part in key]
+        diagonal = [jnp.where(eye, part, 0.0) for part in kk]
+        s_cols = [lax.rsqrt(jnp.sum(part, axis=1, keepdims=True) + EPSILON) for part in diagonal]
+        s_rows = [lax.rsqrt(jnp.sum(part, axis=0, keepdims=True) + EPSILON) for part in diagonal]
+        lowers = []
+        for h in range(HEADS):
+            fade = jnp.where(tril, jnp.exp(jnp.where(tril, c_cols[h] - c_rows[h], 0.0)), 0.0) * s_rows[h // 2]
+            fs[h, block, :] = fade
+            lowers.append(jnp.where(strict, kk[h // 2] * fade * (s_cols[h // 2] * b_cols[h]), 0.0))
+        ts = [t * b_row for t, b_row in zip(unit_inverses(lowers, rows, cols), b_rows)]
+        for h in range(HEADS):
+            tinv[h, block, :] = ts[h]
+        erases = [mm2l(ts[h] * (s_rows[h // 2] * jnp.exp(c_rows[h])), key[h // 2]) for h in range(HEADS)]
+        for h in range(HEADS):
+            ew[h, block, pl.ds(0, D)] = erases[h]
+        takens = [
+            mm2r(key[h // 2], erases[h] * (s_cols[h // 2] * jnp.exp(ends[h] - c_cols[h])), TN)
+            for h in range(HEADS)
+        ]
+        for h in range(HEADS):
+            mc[h, c] = jnp.where(eye, jnp.exp(ends[h]), 0.0) - takens[h]
         return carry
 
     lax.fori_loop(0, CHUNKS, key_body, 0)
@@ -257,11 +309,13 @@
     for h in range(HEADS):
         pre[h, 0, :, left] = identity
         pre[h, 0, :, right] = jnp.zeros((D, D), F32)
-        running = mc[h, 0]
-        for c in range(1, CHUNKS):
-            pre[h, c, :, left] = running
-            running = mm3(mc[h, c], running)
-        m_send[h] = running
+    runnings = [mc[h, 0] for h in range(HEADS)]
+    for c in range(1, CHUNKS):
+        for h in range(HEADS):
+            pre[h, c, :, left] = runnings[h]
+        runnings = [mm3(mc[h, c], runnings[h]) for h in range(HEADS)]
+    for h in range(HEADS):
+        m_send[h] = runnings[h]
 
     def unit_head(u):
         return u // 2
@@ -281,10 +335,15 @@
     m_recv[l] = m_send[unit_head(l)]
 
     v_rim = arrived(copies[4], v_copies, 1, vbuf)
-    rim_arrived(v_rim, vbuf)
     taps_v = wbuf[:, pl.ds(pl.multiple_of(4096 + z * 512, 512), 512)].astype(F32)
 
-    def value_body(c, carry):
+    def value_body(i, carry):
+        c = lax.rem(i + 1, CHUNKS)
+
+        @pl.when(i == CHUNKS - 1)
+        def _():
+            rim_arrived(v_rim, vbuf)
+
         start = pl.multiple_of(c * C, C)
         block = pl.ds(start, C)
         values = conv(vbuf, start, taps_v)
@@ -303,22 +362,26 @@
         return carry
 
     lax.fori_loop(0, CHUNKS, value_body, 0)
+    runnings = [ac[h, 0] for h in range(HEADS)]
+    for c in range(1, CHUNKS):
+        for h in range(HEADS):
+            pre[h, c, :, right] = runnings[h]
+        runnings = [mm3(mc[h, c], runnings[h]) + ac[h, c] for h in range(HEADS)]
     for h in range(HEADS):
-        running = ac[h, 0]
-        for c in range(1, CHUNKS):
-            pre[h, c, :, right] = running
-            running = mm3(mc[h, c], running) + ac[h, c]
-        a_send[h] = running.T
+        a_send[h] = runnings[h].T
     for copy in a_copies:
         copy.start()
     a_recv[l] = a_send[unit_head(l), unit_half(l), :]
 
     for copy in m_copies:
         copy.wait_recv()
-    running = m_recv[0]
+    running, later = m_recv[0], m_recv[LINE - 1]
     for i in range(1, LINE):
         mpre[i] = running
         running = mm3(m_recv[i], running)
+        msuf[LINE - 1 - i] = later
+        if i < LINE - 1:
+            later = mm3(later, m_recv[LINE - 1 - i])
     ym_send[...] = running
     ym_copies, ya_copies = [], []
     for d in range(1, LINES):
@@ -327,12 +390,6 @@
         ya_copies.append(to_seq(9, d, target, ya_send, ya_recv.at[d - 1]))
     for copy in ym_copies:
         copy.start()
-    running = m_recv[LINE - 1]
-    for i in range(LINE - 2, -1, -1):
-        msuf[i] = running
-        if i:
-            running = mm3(running, m_recv[i])
-
     for copy in a_copies:
         copy.wait_recv()
     total = a_recv[LINE - 1]
@@ -364,10 +421,15 @@
     h_recv[l] = h_send[l]
 
     q_rim = arrived(copies[5], q_copies, 2, qbuf)
-    rim_arrived(q_rim, qbuf)
     taps_q = wbuf[:, pl.ds(pl.multiple_of(z * 256, 256), 256)].astype(F32)
 
-    def query_body(c, carry):
+    def query_body(i, carry):
+        c = lax.rem(i + 1, CHUNKS)
+
+        @pl.when(i == CHUNKS - 1)
+        def _():
+            rim_arrived(q_rim, qbuf)
+
         start = pl.multiple_of(c * C, C)
         block = pl.ds(start, C)
         queries = conv(qbuf, start, taps_q)
@@ -409,20 +471,17 @@
     out_rows(z)
     o_recv[z] = o_send[z]
 
-    copies[6].wait()
-    for copy in o_copies:
-        copy.wait_recv()
-    gain = gain_ref[...]
-
-    def norm_body(g, carry):
+    def norm(g):
         for h in range(HEADS):
             a = o_recv[g, :, pl.ds(h * D, D)].astype(F32)
             a = a * lax.rsqrt(jnp.mean(a * a, axis=1, keepdims=True) + EPSILON)
             here = pl.ds(pl.multiple_of(g * 512 + h * D, D), D)
-            out_ref[:, here] = (a * gain * silu(gate[:, here].astype(F32))).astype(BF16)
-        return carry
-
-    lax.fori_loop(0, GROUPS, norm_body, 0)
+            out_ref[:, here] = (a * gating[:, here]).astype(BF16)
+
+    norm(z)
+    for d in (1, 7, 2, 6, 3, 5, 4):
+        o_copies[d - 1].wait_recv()
+        norm(lax.rem(z + GROUPS - d, GROUPS))
 
     for copy in g_copies + k_copies + v_copies + q_copies + [k_rim, v_rim, q_rim]:
         copy.wait_send()
@@ -443,8 +502,9 @@
             pltpu.VMEM((RIM + ROWS, 256), BF16),
             pltpu.VMEM((RIM + ROWS, 512), BF16),
             pltpu.VMEM((TOK, 4096), BF16),
-            pltpu.VMEM((TOK, 32), BF16),
-            pltpu.VMEM((TOK, 32), BF16),
+            pltpu.VMEM((TOK, 4096), F32),
+            pltpu.VMEM((32, TOK), BF16),
+            pltpu.VMEM((32, TOK), BF16),
             pltpu.VMEM((4, 8192), BF16),
             pltpu.VMEM((GROUPS, 8, C), F32),
             pltpu.VMEM((GROUPS, 8, C), F32),
@@ -476,10 +536,10 @@
             pltpu.SemaphoreType.DMA((11, 8)),
         ],
         compiler_params=pltpu.CompilerParams(
-            collective_id=0, has_side_effects=True, vmem_limit_bytes=48 * 1024 * 1024
+            collective_id=0, has_side_effects=True, vmem_limit_bytes=60 * 1024 * 1024
         ),
     )(
-        query_in, key_in, value_in, gate_in, write_strength, log_decay, conv_weight, norm_gain.reshape(1, D)
+        query_in, key_in, value_in, gate_in, write_strength.T, log_decay.T, conv_weight, norm_gain.reshape(1, D)
     )
 
 

time: 103 us -> 74.8 us (0.73)
  Pallas kernels: 95.9 us -> 72.8 us
  local copies, waits for them, and re-layouts: 7.07 us -> 1.87 us
    pallas_call x1, Pallas kernels: 95.9 us -> 72.8 us  [local(): pl.pallas_call(kernel, out_shape=jax.ShapeDtypeStruct((TOK, 4096), BF16),...]
    unnamed x17 -> x1, local copies, waits for them, and re-layouts: 7.07 us -> 1.87 us
where the time goes in v1:
time: 74.8 us; the launch traced here: 74.7 us
  Pallas kernels  72.8 us (97%)
  local copies, waits for them, and re-layouts  1.87 us (2%)
    pallas_call x1, Pallas kernels, local(): pl.pallas_call(kernel, out_shape=jax.ShapeDtypeStruct((TOK, 4096), BF16),...  72.8 us
    unnamed x1, local copies, waits for them, and re-layouts  1.87 us

profile of v1, /device:TPU:1, one launch (start us, length us, event | category | flops | bytes accessed | tf_op | source)
XLA Modules:
  0.0 74.7 jit_solution(6102898818090688002)
XLA Ops:
  0.0 72.8 %shard_map.82 = bf16[64,4096]{1,0:T(8,128)(2,1)} custom-call(bf16[64,2048]{1,0:T(8,128)(2,1)} %q_in.1, bf16[64,2048]{1,0:T(8,128)(2,1)} %k_in.1, bf16[64,4096]{1,0:T(8,128)(2,1)} %v_in.1, bf16[64,4096]{1,0:T(8,128)(2,1)} %gate_in.1, bf16[32,64]{1,0:T(8,128)(2,1)} %bitcast.3, bf16[32,64]{1,0:T(8,128)(2,1)} %bitcast.4, bf16[4,8192]{1,0:T(4,128)(2,1)} %w_in.1, ...), custom_call_target="tpu_custom_call" | custom-call | tf_op jit(solution)/shard_map/pallas_call | solution.py:495
  72.8 1.9 %copy.10 = bf16[64,4096]{1,0:T(8,128)(2,1)} copy(bf16[64,4096]{1,0:T(8,128)(2,1)} %shard_map.82) | data formatting | bytes 1048576

commit v2 on v1

--- a/solution.py
+++ b/solution.py
@@ -23,6 +23,7 @@
 ROWS = TOK * GROUPS
 CHUNKS = ROWS // C
 RIM = 16
+PAIR = 2
 
 NN = (((1,), (0,)), ((), ()))
 NT = (((1,), (1,)), ((), ()))
@@ -65,6 +66,19 @@
     both = dot(a1, beside(b1, b2, dims), dims)
     half = both.shape[1] // 2
     return both[:, :half] + both[:, half:] + dot(a2, b1, dims)
+
+
+def pack_map(m, f_row, eye):
+    sub = lax.broadcasted_iota(jnp.int32, (RIM, D), 0)
+    f1 = f_row.astype(BF16).astype(F32)
+    f2 = (f_row - f1).astype(BF16).astype(F32)
+    pieces = jnp.where(sub == 0, f1, jnp.where(sub == 1, f2, jnp.where(sub == 2, f_row - f1 - f2, 0.0)))
+    return jnp.concatenate([m - jnp.where(eye, f_row, 0.0), pieces], axis=0).astype(BF16)
+
+
+def unpack_map(packed, eye):
+    f_row = jnp.sum(packed[D:].astype(F32), axis=0, keepdims=True)
+    return packed[:D].astype(F32) + jnp.where(eye, f_row, 0.0), f_row
 
 
 def silu(x):
@@ -120,9 +134,9 @@
 def kernel(
     q_in, k_in, v_in, gate_in, ws_in, ld_in, w_in, gain_ref, out_ref,
     qbuf, kbuf, vbuf, gate, gating, ws, ld, wbuf, gb_send, gb_recv,
-    kc, fs, tinv, ew, mc, ac, pre, m_send, a_send, m_recv, a_recv,
-    mpre, msuf, apre, ym_send, ya_send, ym_recv, ya_recv, h_send, h_recv, pb, o_send, o_recv,
-    local_sem, send_sem, recv_sem,
+    kc, fs, tinv, ew, mc, ac, pre, m_send, a_send, m_recv, maps, a_recv,
+    mpre, msuf, mpair, apre, ym_send, ya_send, ym_recv, ya_recv, h_send, h_recv, pb, o_send, o_recv,
+    local_sem, send_sem, recv_sem, rim_sem,
 ):
     s = lax.axis_index("seq")
     z = lax.axis_index("head")
@@ -144,7 +158,9 @@
         pl.semaphore_signal(
             barrier, inc=1, device_id=(lax.rem(y + d, LINES) * LINE + l, z), device_id_type=MESH
         )
-    pl.semaphore_signal(barrier, inc=1, device_id=(lax.rem(s + SEQ - 1, SEQ), z), device_id_type=MESH)
+    pl.semaphore_signal(
+        barrier, inc=1, device_id=(lax.rem(s + SEQ - 1, SEQ), GROUPS - 1), device_id_type=MESH
+    )
 
     mine = pl.ds(pl.multiple_of(RIM + z * TOK, RIM), TOK)
 
@@ -169,17 +185,15 @@
     tril = rows >= cols
     strict = rows > cols
 
-    copies[0].wait()
-    copies[1].wait()
-    upto = jnp.where(rows <= cols, 1.0, 0.0)[:TOK, :TOK].astype(BF16)
-    running = dot(ld[...], upto)
-    both = jnp.concatenate([ws[...].astype(F32), running], axis=0)
-    both = jnp.concatenate([both, both], axis=1)
-    for g in range(GROUPS):
-        gb_send[g] = jnp.concatenate(
-            [both[HEADS * g : HEADS * g + HEADS], both[32 + HEADS * g : 32 + HEADS * g + HEADS]], axis=0
-        )
-    pl.semaphore_wait(barrier, GROUPS - 1 + LINE - 1 + LINES - 1 + 1)
+    partners = GROUPS - 1 + LINE - 1 + LINES - 1
+
+    @pl.when(z < GROUPS - 1)
+    def _():
+        pl.semaphore_wait(barrier, partners)
+
+    @pl.when(z == GROUPS - 1)
+    def _():
+        pl.semaphore_wait(barrier, partners + GROUPS)
 
     def to_head(kind, d, src, dst):
         return pltpu.make_async_remote_copy(
@@ -204,16 +218,52 @@
     def columns_to(d, width):
         return pl.ds(pl.multiple_of(at_head(d) * width, width), width)
 
-    order = [4, 3, 5, 2, 6, 1, 7]
-    k_copies, v_copies, q_copies, g_copies = [], [], [], []
-    for d in order:
-        g_copies.append(to_head(0, d, gb_send.at[at_head(d)], gb_recv.at[z]))
-        k_copies.append(to_head(1, d, k_in.at[:, columns_to(d, 256)], kbuf.at[mine, :]))
-    for d in order:
-        v_copies.append(to_head(2, d, v_in.at[:, columns_to(d, 512)], vbuf.at[mine, :]))
-    for d in order:
-        q_copies.append(to_head(3, d, q_in.at[:, columns_to(d, 256)], qbuf.at[mine, :]))
-    for copy in g_copies + k_copies + v_copies + q_copies:
+    near = [1, 7, 2, 6, 3, 5, 4]
+    k_copies = [to_head(1, d, k_in.at[:, columns_to(d, 256)], kbuf.at[mine, :]) for d in near]
+    v_copies = [to_head(2, d, v_in.at[:, columns_to(d, 512)], vbuf.at[mine, :]) for d in near]
+    q_copies = [to_head(3, d, q_in.at[:, columns_to(d, 256)], qbuf.at[mine, :]) for d in near]
+    g_copies = [to_head(0, d, gb_send.at[at_head(d)], gb_recv.at[z]) for d in near]
+    following = lax.rem(s + 1, SEQ)
+
+    def rim_copies(index, source, buf, width):
+        return [
+            pltpu.make_async_remote_copy(
+                src_ref=source.at[pl.ds(TOK - RIM, RIM), pl.ds(g * width, width)],
+                dst_ref=buf.at[pl.ds(0, RIM), :],
+                send_sem=rim_sem.at[index, g],
+                recv_sem=recv_sem.at[4, index],
+                device_id=(following, g),
+                device_id_type=MESH,
+            )
+            for g in range(GROUPS)
+        ]
+
+    k_rims = rim_copies(0, k_in, kbuf, 256)
+    v_rims = rim_copies(1, v_in, vbuf, 512)
+    q_rims = rim_copies(2, q_in, qbuf, 256)
+
+    def start_rims(rims):
+        @pl.when(z == GROUPS - 1)
+        def _():
+            for rim in rims:
+                rim.start()
+
+    start_rims(k_rims)
+    for copy in k_copies:
+        copy.start()
+
+    copies[0].wait()
+    copies[1].wait()
+    upto = jnp.where(rows <= cols, 1.0, 0.0)[:TOK, :TOK].astype(BF16)
+    sums = dot(ld[...], upto)
+    both = jnp.concatenate([ws[...].astype(F32), sums], axis=0)
+    both = jnp.concatenate([both, both], axis=1)
+    for g in range(GROUPS):
+        gb_send[g] = jnp.concatenate(
+            [both[HEADS * g : HEADS * g + HEADS], both[32 + HEADS * g : 32 + HEADS * g + HEADS]], axis=0
+        )
+    start_rims(v_rims)
+    for copy in g_copies + v_copies:
         copy.start()
     gb_recv[z] = gb_send[z]
 
@@ -227,18 +277,10 @@
 
     lax.fori_loop(0, GROUPS, gate_body, 0)
 
-    following = lax.rem(s + 1, SEQ)
-
-    def rim_copy(index, buf):
-        return to_seq(4, index, following, buf.at[pl.ds(ROWS, RIM), :], buf.at[pl.ds(0, RIM), :])
-
-    def arrived(own, others, index, buf):
+    def arrived(own, others):
         own.wait()
         for copy in others:
             copy.wait_recv()
-        rim = rim_copy(index, buf)
-        rim.start()
-        return rim
 
     def rim_arrived(rim, buf):
         rim.wait_recv()
@@ -258,51 +300,52 @@
     copies[2].wait()
     for copy in g_copies:
         copy.wait_recv()
-    k_rim = arrived(copies[3], k_copies, 0, kbuf)
+    arrived(copies[3], k_copies)
     taps_k = wbuf[:, pl.ds(pl.multiple_of(2048 + z * 256, 256), 256)].astype(F32)
 
     def key_body(i, carry):
-        c = lax.rem(i + 1, CHUNKS)
-
-        @pl.when(i == CHUNKS - 1)
+        @pl.when(i == CHUNKS // PAIR - 1)
         def _():
-            rim_arrived(k_rim, kbuf)
-
-        start = pl.multiple_of(c * C, C)
-        block = pl.ds(start, C)
-        keys = conv(kbuf, start, taps_k)
-        kc[block, :] = keys
-        across, down = chunk_scales(c)
-        b_cols = [down[:, h : h + 1] for h in range(HEADS)]
-        c_cols = [down[:, HEADS + h : HEADS + h + 1] for h in range(HEADS)]
-        b_rows = [across[h : h + 1] for h in range(HEADS)]
-        c_rows = [across[HEADS + h : HEADS + h + 1] for h in range(HEADS)]
-        ends = [c_row[:, C - 1 : C] for c_row in c_rows]
-        key = [keys[:, kh * D : (kh + 1) * D] for kh in range(2)]
-        kk = [dot(part, part, NT) for part in key]
-        diagonal = [jnp.where(eye, part, 0.0) for part in kk]
-        s_cols = [lax.rsqrt(jnp.sum(part, axis=1, keepdims=True) + EPSILON) for part in diagonal]
-        s_rows = [lax.rsqrt(jnp.sum(part, axis=0, keepdims=True) + EPSILON) for part in diagonal]
-        lowers = []
-        for h in range(HEADS):
-            fade = jnp.where(tril, jnp.exp(jnp.where(tril, c_cols[h] - c_rows[h], 0.0)), 0.0) * s_rows[h // 2]
-            fs[h, block, :] = fade
-            lowers.append(jnp.where(strict, kk[h // 2] * fade * (s_cols[h // 2] * b_cols[h]), 0.0))
-        ts = [t * b_row for t, b_row in zip(unit_inverses(lowers, rows, cols), b_rows)]
-        for h in range(HEADS):
-            tinv[h, block, :] = ts[h]
-        erases = [mm2l(ts[h] * (s_rows[h // 2] * jnp.exp(c_rows[h])), key[h // 2]) for h in range(HEADS)]
-        for h in range(HEADS):
-            ew[h, block, pl.ds(0, D)] = erases[h]
-        takens = [
-            mm2r(key[h // 2], erases[h] * (s_cols[h // 2] * jnp.exp(ends[h] - c_cols[h])), TN)
-            for h in range(HEADS)
-        ]
-        for h in range(HEADS):
-            mc[h, c] = jnp.where(eye, jnp.exp(ends[h]), 0.0) - takens[h]
+            rim_arrived(k_rims[0], kbuf)
+
+        units = []
+        for n in range(PAIR):
+            c = lax.rem(i * PAIR + PAIR + n, CHUNKS)
+            start = pl.multiple_of(c * C, C)
+            keys = conv(kbuf, start, taps_k)
+            kc[pl.ds(start, C), :] = keys
+            across, down = chunk_scales(c)
+            for kh in range(2):
+                key = keys[:, kh * D : (kh + 1) * D]
+                kk = dot(key, key, NT)
+                diagonal = jnp.where(eye, kk, 0.0)
+                s_col = lax.rsqrt(jnp.sum(diagonal, axis=1, keepdims=True) + EPSILON)
+                s_row = lax.rsqrt(jnp.sum(diagonal, axis=0, keepdims=True) + EPSILON)
+                for j in range(2):
+                    h = kh * 2 + j
+                    b_col, c_col = down[:, h : h + 1], down[:, HEADS + h : HEADS + h + 1]
+                    b_row, c_row = across[h : h + 1], across[HEADS + h : HEADS + h + 1]
+                    end = c_row[:, C - 1 : C]
+                    fade = jnp.where(tril, jnp.exp(jnp.where(tril, c_col - c_row, 0.0)), 0.0) * s_row
+                    fs[h, pl.ds(start, C), :] = fade
+                    lower = jnp.where(strict, kk * fade * (s_col * b_col), 0.0)
+                    units.append((
+                        h, c, pl.ds(start, C), key, lower, b_row, s_row * jnp.exp(c_row),
+                        s_col * jnp.exp(end - c_col), jnp.exp(end),
+                    ))
+        ts = unit_inverses([unit[4] for unit in units], rows, cols)
+        ts = [t * unit[5] for t, unit in zip(ts, units)]
+        for t, unit in zip(ts, units):
+            tinv[unit[0], unit[2], :] = t
+        erases = [mm2l(t * unit[6], unit[3]) for t, unit in zip(ts, units)]
+        for erase, unit in zip(erases, units):
+            ew[unit[0], unit[2], pl.ds(0, D)] = erase
+        takens = [mm2r(unit[3], erase * unit[7], TN) for erase, unit in zip(erases, units)]
+        for taken, unit in zip(takens, units):
+            mc[unit[0], unit[1]] = jnp.where(eye, unit[8], 0.0) - taken
         return carry
 
-    lax.fori_loop(0, CHUNKS, key_body, 0)
+    lax.fori_loop(0, CHUNKS // PAIR, key_body, 0)
 
     identity = jnp.where(eye, 1.0, 0.0)
     left, right = pl.ds(0, D), pl.ds(D, D)
@@ -315,7 +358,10 @@
             pre[h, c, :, left] = runnings[h]
         runnings = [mm3(mc[h, c], runnings[h]) for h in range(HEADS)]
     for h in range(HEADS):
-        m_send[h] = runnings[h]
+        decay = gb_recv[0, HEADS + h : HEADS + h + 1, TOK - 1 : TOK]
+        for g in range(1, GROUPS):
+            decay = decay + gb_recv[g, HEADS + h : HEADS + h + 1, TOK - 1 : TOK]
+        m_send[h] = pack_map(runnings[h], jnp.broadcast_to(jnp.exp(decay), (1, D)), eye)
 
     def unit_head(u):
         return u // 2
@@ -330,97 +376,120 @@
         m_copies.append(to_seq(5, d, target, m_send.at[unit_head(u)], m_recv.at[l]))
         a_copies.append(to_seq(6, d, target, a_send.at[unit_head(u), unit_half(u), :], a_recv.at[l]))
         h_copies.append(to_seq(7, d, target, h_send.at[u], h_recv.at[l]))
-    for copy in m_copies:
+    start_rims(q_rims)
+    for copy in m_copies + q_copies:
         copy.start()
     m_recv[l] = m_send[unit_head(l)]
 
-    v_rim = arrived(copies[4], v_copies, 1, vbuf)
+    arrived(copies[4], v_copies)
     taps_v = wbuf[:, pl.ds(pl.multiple_of(4096 + z * 512, 512), 512)].astype(F32)
 
     def value_body(i, carry):
-        c = lax.rem(i + 1, CHUNKS)
-
-        @pl.when(i == CHUNKS - 1)
+        @pl.when(i == CHUNKS // PAIR - 1)
         def _():
-            rim_arrived(v_rim, vbuf)
-
-        start = pl.multiple_of(c * C, C)
-        block = pl.ds(start, C)
-        values = conv(vbuf, start, taps_v)
-        across, down = chunk_scales(c)
-        for kh in range(2):
-            key = kc[block, pl.ds(kh * D, D)]
-            key32 = key.astype(F32)
-            s_col = lax.rsqrt(jnp.sum(key32 * key32, axis=1, keepdims=True) + EPSILON)
-            for j in range(2):
-                h = kh * 2 + j
-                c_col = down[:, HEADS + h : HEADS + h + 1]
-                end = across[HEADS + h : HEADS + h + 1, C - 1 : C]
-                write = mm2l(tinv[h, block, :], values[:, h * D : (h + 1) * D])
-                ew[h, block, pl.ds(D, D)] = write
-                ac[h, c] = mm2r(key, write * (s_col * jnp.exp(end - c_col)), TN)
+            rim_arrived(v_rims[0], vbuf)
+
+        for n in range(PAIR):
+            c = lax.rem(i * PAIR + PAIR + n, CHUNKS)
+            start = pl.multiple_of(c * C, C)
+            block = pl.ds(start, C)
+            values = conv(vbuf, start, taps_v)
+            across, down = chunk_scales(c)
+            for kh in range(2):
+                key = kc[block, pl.ds(kh * D, D)]
+                key32 = key.astype(F32)
+                s_col = lax.rsqrt(jnp.sum(key32 * key32, axis=1, keepdims=True) + EPSILON)
+                for j in range(2):
+                    h = kh * 2 + j
+                    c_col = down[:, HEADS + h : HEADS + h + 1]
+                    end = across[HEADS + h : HEADS + h + 1, C - 1 : C]
+                    write = mm2l(tinv[h, block, :], values[:, h * D : (h + 1) * D])
+                    ew[h, block, pl.ds(D, D)] = write
+                    ac[h, c] = mm2r(key, write * (s_col * jnp.exp(end - c_col)), TN)
         return carry
 
-    lax.fori_loop(0, CHUNKS, value_body, 0)
+    lax.fori_loop(0, CHUNKS // PAIR, value_body, 0)
     runnings = [ac[h, 0] for h in range(HEADS)]
     for c in range(1, CHUNKS):
         for h in range(HEADS):
             pre[h, c, :, right] = runnings[h]
         runnings = [mm3(mc[h, c], runnings[h]) + ac[h, c] for h in range(HEADS)]
     for h in range(HEADS):
-        a_send[h] = runnings[h].T
+        a_send[h] = runnings[h].T.astype(BF16)
     for copy in a_copies:
         copy.start()
     a_recv[l] = a_send[unit_head(l), unit_half(l), :]
 
     for copy in m_copies:
         copy.wait_recv()
-    running, later = m_recv[0], m_recv[LINE - 1]
-    for i in range(1, LINE):
-        mpre[i] = running
-        running = mm3(m_recv[i], running)
-        msuf[LINE - 1 - i] = later
-        if i < LINE - 1:
-            later = mm3(later, m_recv[LINE - 1 - i])
-    ym_send[...] = running
+    m, f_total = [], None
+    for i in range(LINE):
+        unpacked, f_row = unpack_map(m_recv[i], eye)
+        maps[i] = unpacked
+        m.append(unpacked)
+        f_total = f_row if f_total is None else f_total * f_row
+    m01, m23, m45, m67 = mm3(m[1], m[0]), mm3(m[3], m[2]), mm3(m[5], m[4]), mm3(m[7], m[6])
+    m03, m47 = mm3(m23, m01), mm3(m67, m45)
+    m12, m46 = mm3(m23, m[1]), mm3(m[6], m45)
+    ym_send[...] = pack_map(mm3(m47, m03), f_total, eye)
+    mpre[1], mpre[2], mpre[3], mpre[4] = m[0], m01, mm3(m[2], m01), m03
+    mpre[5], mpre[6], mpre[7] = mm3(m[4], m03), mm3(m45, m03), mm3(m46, m03)
+    msuf[6], msuf[5], msuf[4], msuf[3] = m[7], m67, mm3(m67, m[5]), m47
+    msuf[2], msuf[1], msuf[0] = mm3(m47, m[3]), mm3(m47, m23), mm3(m47, m12)
+    mpair[0], mpair[1] = m23, m45
     ym_copies, ya_copies = [], []
     for d in range(1, LINES):
         target = lax.rem(y + d, LINES) * LINE + l
         ym_copies.append(to_seq(8, d, target, ym_send, ym_recv.at[d - 1]))
         ya_copies.append(to_seq(9, d, target, ya_send, ya_recv.at[d - 1]))
-    for copy in ym_copies:
-        copy.start()
+
+    def start_later(across):
+        for d in range(1, LINES):
+
+            @pl.when(y + d < LINES)
+            def _(d=d):
+                across[d - 1].start()
+
+    def wait_earlier(across):
+        for d in range(1, LINES):
+
+            @pl.when(y >= d)
+            def _(d=d):
+                across[d - 1].wait_recv()
+
+    start_later(ym_copies)
     for copy in a_copies:
         copy.wait_recv()
-    total = a_recv[LINE - 1]
+    adds = [a_recv[i] for i in range(LINE)]
+    total = adds[LINE - 1].astype(F32)
     for i in range(LINE - 1):
-        total = total + mm3(a_recv[i], msuf[i], NT)
+        total = total + mm2r(adds[i], msuf[i], NT)
     ya_send[...] = total
-    for copy in ya_copies:
-        copy.start()
-
-    running = a_recv[0]
+    start_later(ya_copies)
+
+    apre[1] = adds[0].astype(F32)
+    apre[2] = mm2r(adds[0], maps[1], NT) + adds[1].astype(F32)
+    apre[3] = mm3(apre[2], maps[2], NT) + adds[2].astype(F32)
+    apre[4] = mm3(apre[2], mpair[0], NT) + (mm2r(adds[2], maps[3], NT) + adds[3].astype(F32))
+    apre[5] = mm3(apre[4], maps[4], NT) + adds[4].astype(F32)
+    apre[6] = mm3(apre[4], mpair[1], NT) + (mm2r(adds[4], maps[5], NT) + adds[5].astype(F32))
+    apre[7] = mm3(apre[6], maps[6], NT) + adds[6].astype(F32)
+
+    wait_earlier(ym_copies)
+    line_one = jnp.where(y >= 1, unpack_map(ym_recv[0], eye)[0], 0.0)
+    line_two = jnp.where(y >= 2, mm3(line_one, unpack_map(ym_recv[1], eye)[0]), 0.0)
+    wait_earlier(ya_copies)
+    entering = jnp.where(y >= 1, ya_recv[0], 0.0)
+    entering = entering + jnp.where(y >= 2, mm3(ya_recv[1], line_one, NT), 0.0)
+    entering = entering + jnp.where(y >= 3, mm3(ya_recv[2], line_two, NT), 0.0)
+    h_send[0] = entering.astype(BF16)
     for i in range(1, LINE):
-        apre[i] = running
-        if i < LINE - 1:
-            running = mm3(running, m_recv[i], NT) + a_recv[i]
-
-    for copy in ym_copies:
-        copy.wait_recv()
-    across_two = mm3(ym_recv[0], ym_recv[1])
-    for copy in ya_copies:
-        copy.wait_recv()
-    entering = jnp.where(y >= 1, ya_recv[0], 0.0)
-    entering = entering + jnp.where(y >= 2, mm3(ya_recv[1], ym_recv[0], NT), 0.0)
-    entering = entering + jnp.where(y >= 3, mm3(ya_recv[2], across_two, NT), 0.0)
-    h_send[0] = entering
-    for i in range(1, LINE):
-        h_send[i] = mm3(entering, mpre[i], NT) + apre[i]
+        h_send[i] = (mm3(entering, mpre[i], NT) + apre[i]).astype(BF16)
     for copy in h_copies:
         copy.start()
     h_recv[l] = h_send[l]
 
-    q_rim = arrived(copies[5], q_copies, 2, qbuf)
+    arrived(copies[5], q_copies)
     taps_q = wbuf[:, pl.ds(pl.multiple_of(z * 256, 256), 256)].astype(F32)
 
     def query_body(i, carry):
@@ -428,7 +497,7 @@
 
         @pl.when(i == CHUNKS - 1)
         def _():
-            rim_arrived(q_rim, qbuf)
+            rim_arrived(q_rims[0], qbuf)
 
         start = pl.multiple_of(c * C, C)
         block = pl.ds(start, C)
@@ -454,18 +523,17 @@
 
     for copy in h_copies:
         copy.wait_recv()
-    o_copies = []
-    for d in range(1, GROUPS):
-        o_copies.append(to_head(10, d, o_send.at[at_head(d)], o_recv.at[z]))
+    far = [4, 3, 5, 2, 6, 1, 7]
+    o_copies = [to_head(10, d, o_send.at[at_head(d)], o_recv.at[z]) for d in far]
 
     def out_rows(t):
         block = pl.ds(pl.multiple_of(t * TOK, TOK), TOK)
         for h in range(HEADS):
             state = jnp.concatenate([h_recv[2 * h], h_recv[2 * h + 1]], axis=0)
-            o = mm3(pb[h, block, left], state, NT) + pb[h, block, right]
+            o = mm2l(pb[h, block, left], state, NT) + pb[h, block, right]
             o_send[t, :, pl.ds(h * D, D)] = o.astype(BF16)
 
-    for copy, d in zip(o_copies, range(1, GROUPS)):
+    for copy, d in zip(o_copies, far):
         out_rows(at_head(d))
         copy.start()
     out_rows(z)
@@ -479,14 +547,24 @@
             out_ref[:, here] = (a * gating[:, here]).astype(BF16)
 
     norm(z)
-    for d in (1, 7, 2, 6, 3, 5, 4):
-        o_copies[d - 1].wait_recv()
+    for copy, d in zip(o_copies, far):
+        copy.wait_recv()
         norm(lax.rem(z + GROUPS - d, GROUPS))
 
-    for copy in g_copies + k_copies + v_copies + q_copies + [k_rim, v_rim, q_rim]:
+    for copy in g_copies + k_copies + v_copies + q_copies + m_copies + a_copies + h_copies + o_copies:
         copy.wait_send()
-    for copy in m_copies + a_copies + h_copies + ym_copies + ya_copies + o_copies:
-        copy.wait_send()
+
+    @pl.when(z == GROUPS - 1)
+    def _():
+        for rim in k_rims + v_rims + q_rims:
+            rim.wait_send()
+
+    for d in range(1, LINES):
+
+        @pl.when(y + d < LINES)
+        def _(d=d):
+            ym_copies[d - 1].wait_send()
+            ya_copies[d - 1].wait_send()
 
 
 def local(query_in, key_in, value_in, gate_in, write_strength, log_decay, conv_weight, norm_gain):
@@ -515,25 +593,28 @@
             pltpu.VMEM((HEADS, CHUNKS, D, D), F32),
             pltpu.VMEM((HEADS, CHUNKS, D, D), F32),
             pltpu.VMEM((HEADS, CHUNKS, D, 2 * D), F32),
-            pltpu.VMEM((HEADS, D, D), F32),
-            pltpu.VMEM((HEADS, D, D), F32),
+            pltpu.VMEM((HEADS, D + RIM, D), BF16),
+            pltpu.VMEM((HEADS, D, D), BF16),
+            pltpu.VMEM((LINE, D + RIM, D), BF16),
             pltpu.VMEM((LINE, D, D), F32),
-            pltpu.VMEM((LINE, 64, D), F32),
+            pltpu.VMEM((LINE, 64, D), BF16),
             pltpu.VMEM((LINE, D, D), F32),
             pltpu.VMEM((LINE, D, D), F32),
+            pltpu.VMEM((2, D, D), F32),
             pltpu.VMEM((LINE, 64, D), F32),
-            pltpu.VMEM((D, D), F32),
+            pltpu.VMEM((D + RIM, D), BF16),
             pltpu.VMEM((64, D), F32),
-            pltpu.VMEM((LINES - 1, D, D), F32),
+            pltpu.VMEM((LINES - 1, D + RIM, D), BF16),
             pltpu.VMEM((LINES - 1, 64, D), F32),
-            pltpu.VMEM((LINE, 64, D), F32),
-            pltpu.VMEM((LINE, 64, D), F32),
+            pltpu.VMEM((LINE, 64, D), BF16),
+            pltpu.VMEM((LINE, 64, D), BF16),
             pltpu.VMEM((HEADS, ROWS, 2 * D), F32),
             pltpu.VMEM((GROUPS, TOK, 512), BF16),
             pltpu.VMEM((GROUPS, TOK, 512), BF16),
             pltpu.SemaphoreType.DMA((7,)),
             pltpu.SemaphoreType.DMA((11, 8)),
             pltpu.SemaphoreType.DMA((11, 8)),
+            pltpu.SemaphoreType.DMA((3, 8)),
         ],
         compiler_params=pltpu.CompilerParams(
             collective_id=0, has_side_effects=True, vmem_limit_bytes=60 * 1024 * 1024

time: 74.8 us -> 65.6 us (0.88)
  the two profiles are of different devices: /device:TPU:1 before, /device:TPU:49 now
where the time goes in v2:
time: 65.6 us; the launch traced here: 65.4 us
  Pallas kernels  63.6 us (97%)
  local copies, waits for them, and re-layouts  1.87 us (3%)
    pallas_call x1, Pallas kernels, local(): pl.pallas_call(kernel, out_shape=jax.ShapeDtypeStruct((TOK, 4096), BF16),...  63.6 us
    unnamed x1, local copies, waits for them, and re-layouts  1.87 us

profile of v2, /device:TPU:49, one launch (start us, length us, event | category | flops | bytes accessed | tf_op | source)
XLA Modules:
  0.0 65.4 jit_solution(4341646089253738780)
XLA Ops:
  0.0 63.6 %shard_map.82 = bf16[64,4096]{1,0:T(8,128)(2,1)} custom-call(bf16[64,2048]{1,0:T(8,128)(2,1)} %q_in.1, bf16[64,2048]{1,0:T(8,128)(2,1)} %k_in.1, bf16[64,4096]{1,0:T(8,128)(2,1)} %v_in.1, bf16[64,4096]{1,0:T(8,128)(2,1)} %gate_in.1, bf16[32,64]{1,0:T(8,128)(2,1)} %bitcast.3, bf16[32,64]{1,0:T(8,128)(2,1)} %bitcast.4, bf16[4,8192]{1,0:T(4,128)(2,1)} %w_in.1, ...), custom_call_target="tpu_custom_call" | custom-call | tf_op jit(solution)/shard_map/pallas_call | solution.py:573
  63.6 1.9 %copy.10 = bf16[64,4096]{1,0:T(8,128)(2,1)} copy(bf16[64,4096]{1,0:T(8,128)(2,1)} %shard_map.82) | data formatting | bytes 1048576

commit v3 on v2

--- a/solution.py
+++ b/solution.py
@@ -370,7 +370,7 @@
         return pl.ds(pl.multiple_of(lax.rem(u, 2) * 64, 64), 64)
 
     m_copies, a_copies, h_copies = [], [], []
-    for d in range(1, LINE):
+    for d in [2, 6, 4, 3, 5, 1, 7]:
         u = at_line(d)
         target = y * LINE + u
         m_copies.append(to_seq(5, d, target, m_send.at[unit_head(u)], m_recv.at[l]))
@@ -523,8 +523,12 @@
 
     for copy in h_copies:
         copy.wait_recv()
-    far = [4, 3, 5, 2, 6, 1, 7]
-    o_copies = [to_head(10, d, o_send.at[at_head(d)], o_recv.at[z]) for d in far]
+    def far(i):
+        half = i // 2
+        return 4 + half - lax.rem(i, 2) * ((i + 1) // 2 + half)
+
+    def out_copy(d):
+        return to_head(10, d, o_send.at[at_head(d)], o_recv.at[z])
 
     def out_rows(t):
         block = pl.ds(pl.multiple_of(t * TOK, TOK), TOK)
@@ -533,10 +537,17 @@
             o = mm2l(pb[h, block, left], state, NT) + pb[h, block, right]
             o_send[t, :, pl.ds(h * D, D)] = o.astype(BF16)
 
-    for copy, d in zip(o_copies, far):
+    def out_body(i, carry):
+        d = far(i)
         out_rows(at_head(d))
-        copy.start()
-    out_rows(z)
+
+        @pl.when(i < GROUPS - 1)
+        def _():
+            out_copy(d).start()
+
+        return carry
+
+    lax.fori_loop(0, GROUPS, out_body, 0)
     o_recv[z] = o_send[z]
 
     def norm(g):
@@ -546,12 +557,24 @@
             here = pl.ds(pl.multiple_of(g * 512 + h * D, D), D)
             out_ref[:, here] = (a * gating[:, here]).astype(BF16)
 
-    norm(z)
-    for copy, d in zip(o_copies, far):
-        copy.wait_recv()
+    def norm_body(i, carry):
+        d = far(lax.rem(i + GROUPS - 1, GROUPS))
+
+        @pl.when(i > 0)
+        def _():
+            out_copy(d).wait_recv()
+
         norm(lax.rem(z + GROUPS - d, GROUPS))
-
-    for copy in g_copies + k_copies + v_copies + q_copies + m_copies + a_copies + h_copies + o_copies:
+        return carry
+
+    lax.fori_loop(0, GROUPS, norm_body, 0)
+
+    def sent_body(i, carry):
+        out_copy(far(i)).wait_send()
+        return carry
+
+    lax.fori_loop(0, GROUPS - 1, sent_body, 0)
+    for copy in g_copies + k_copies + v_copies + q_copies + m_copies + a_copies + h_copies:
         copy.wait_send()
 
     @pl.when(z == GROUPS - 1)

time: 65.6 us -> 65.4 us (level)
  no operation moved by 1% of the time
where the time goes in v3:
time: 65.4 us; the launch traced here: 65.3 us
  Pallas kernels  63.4 us (97%)
  local copies, waits for them, and re-layouts  1.87 us (3%)
    pallas_call x1, Pallas kernels, local(): pl.pallas_call(kernel, out_shape=jax.ShapeDtypeStruct((TOK, 4096), BF16),...  63.4 us
    unnamed x1, local copies, waits for them, and re-layouts  1.87 us

profile of v3, /device:TPU:49, one launch (start us, length us, event | category | flops | bytes accessed | tf_op | source)
XLA Modules:
  0.0 65.3 jit_solution(14910601399442892374)
XLA Ops:
  0.0 63.4 %shard_map.82 = bf16[64,4096]{1,0:T(8,128)(2,1)} custom-call(bf16[64,2048]{1,0:T(8,128)(2,1)} %q_in.1, bf16[64,2048]{1,0:T(8,128)(2,1)} %k_in.1, bf16[64,4096]{1,0:T(8,128)(2,1)} %v_in.1, bf16[64,4096]{1,0:T(8,128)(2,1)} %gate_in.1, bf16[32,64]{1,0:T(8,128)(2,1)} %bitcast.3, bf16[32,64]{1,0:T(8,128)(2,1)} %bitcast.4, bf16[4,8192]{1,0:T(4,128)(2,1)} %w_in.1, ...), custom_call_target="tpu_custom_call" | custom-call | tf_op jit(solution)/shard_map/pallas_call | solution.py:596
  63.4 1.9 %copy.10 = bf16[64,4096]{1,0:T(8,128)(2,1)} copy(bf16[64,4096]{1,0:T(8,128)(2,1)} %shard_map.82) | data formatting | bytes 1048576

commit v4 on v3

--- a/solution.py
+++ b/solution.py
@@ -176,7 +176,7 @@
         pltpu.make_async_copy(q_in.at[:, own_columns(256)], qbuf.at[mine, :], local_sem.at[5]),
         pltpu.make_async_copy(gate_in, gate, local_sem.at[6]),
     ]
-    for copy in copies:
+    for copy in copies[:4]:
         copy.start()
 
     rows = lax.broadcasted_iota(jnp.int32, (C, C), 0)
@@ -250,6 +250,8 @@
 
     start_rims(k_rims)
     for copy in k_copies:
+        copy.start()
+    for copy in copies[4:]:
         copy.start()
 
     copies[0].wait()

time: 65.4 us -> 65.4 us (level)
  no operation moved by 1% of the time
where the time goes in v4:
time: 65.4 us; the launch traced here: 65.3 us
  Pallas kernels  63.4 us (97%)
  local copies, waits for them, and re-layouts  1.87 us (3%)
    pallas_call x1, Pallas kernels, local(): pl.pallas_call(kernel, out_shape=jax.ShapeDtypeStruct((TOK, 4096), BF16),...  63.4 us
    unnamed x1, local copies, waits for them, and re-layouts  1.87 us

profile of v4, /device:TPU:49, one launch (start us, length us, event | category | flops | bytes accessed | tf_op | source)
XLA Modules:
  0.0 65.3 jit_solution(1911753937405651610)
XLA Ops:
  0.0 63.4 %shard_map.82 = bf16[64,4096]{1,0:T(8,128)(2,1)} custom-call(bf16[64,2048]{1,0:T(8,128)(2,1)} %q_in.1, bf16[64,2048]{1,0:T(8,128)(2,1)} %k_in.1, bf16[64,4096]{1,0:T(8,128)(2,1)} %v_in.1, bf16[64,4096]{1,0:T(8,128)(2,1)} %gate_in.1, bf16[32,64]{1,0:T(8,128)(2,1)} %bitcast.3, bf16[32,64]{1,0:T(8,128)(2,1)} %bitcast.4, bf16[4,8192]{1,0:T(4,128)(2,1)} %w_in.1, ...), custom_call_target="tpu_custom_call" | custom-call | tf_op jit(solution)/shard_map/pallas_call | solution.py:598
  63.4 1.9 %copy.10 = bf16[64,4096]{1,0:T(8,128)(2,1)} copy(bf16[64,4096]{1,0:T(8,128)(2,1)} %shard_map.82) | data formatting | bytes 1048576
